TPU v7x, 32 devices: a whole 2x2x4 slice. The times are simulated.
32 devices in a mesh: group: 2 (over y), ep: 4 (over x, core), side: 4 (over z).
Axes of the slice: x: 2, y: 2, z: 4, core: 2. Of those that a mesh axis runs over, the one named last changes fastest.
Arguments:
- queries: bfloat16 [64, 128, 576], P(('group', 'ep', 'side')), parts along dimension 0, may hold values from -6 to 6
- cache: bfloat16 [64, 256, 576], P(('group', 'ep', 'side')), parts along dimension 0, may hold values from -6 to 6
- lengths: int32 [64], P(('group', 'ep', 'side')), parts along dimension 0, may hold values from 2 to 256, as said below
- resid: bfloat16 [64, 7168], P(('group', 'ep', 'side')), parts along dimension 0, may hold values from -6 to 6
- uv_weight: bfloat16 [128, 512, 128], P(('ep', 'side')), may hold values from -0.25 to 0.25
- out_weight: bfloat16 [16384, 7168], P(('ep', 'side')), may hold values from -0.046875 to 0.046875
- norm_gain: bfloat16 [7168], replicated, may hold values from 0.5 to 1.5
- expert_ids: int32 [64, 2], P(('group', 'ep', 'side')), parts along dimension 0, may hold values from 0 to 3, all different within a row; in each aligned block of 2 rows (0 to 1, 2 to 3, ...) at most 2 rows name the same one
- route_weights: float32 [64, 2], P(('group', 'ep', 'side')), parts along dimension 0, may hold values from 0.1 to 1
- gate_weight: bfloat16 [4, 7168, 2048], P('ep', None, 'side'), may hold values from -0.0625 to 0.0625
- up_weight: bfloat16 [4, 7168, 2048], P('ep', None, 'side'), may hold values from -0.0625 to 0.0625
- down_weight: bfloat16 [4, 2048, 7168], P('ep', 'side'), may hold values from -0.125 to 0.125
Outputs:
- layer_out: bfloat16 [64, 7168], P(('group', 'ep', 'side')), parts along dimension 0
There are 2 independent parts, one for each index of `group`. A program takes and returns all parts, laid end to end along the dimension named above; an argument that names none is the same for every part. Nothing has to cross between parts.
Inputs may be any that keep to these rules, and one draw needn't show every extreme that they name: `lengths`: the used slots of a row are its first ones; some row uses all 256. `expert_ids`: each row names 2 different experts.
All inputs are finite; a program needn't handle non-finite values.
Results may differ from a plain program's by a relative error of at most 0.0075.
Values may be sent and summed in bfloat16 or wider, within the bound.
A program may use at most 128 MiB of HBM per device.

v0:
```python
import jax
import jax.numpy as jnp
from jax import lax
from jax.sharding import PartitionSpec as P


def on_device(
    queries,
    cache,
    lengths,
    resid,
    uv_weight,
    out_weight,
    norm_gain,
    expert_ids,
    route_weights,
    gate_weight,
    up_weight,
    down_weight,
):
    rows_here = queries.shape[0]
    slot_count = cache.shape[1]
    latent_size = uv_weight.shape[1]
    heads_here = uv_weight.shape[0]
    value_size = uv_weight.shape[2]
    scale = 1.0 / 192.0**0.5
    scores = jnp.einsum("rhk,rtk->rht", queries, cache, preferred_element_type=jnp.float32) * scale
    slots = jnp.arange(slot_count, dtype=jnp.int32)
    valid = slots[None, None, :] < lengths[:, None, None]
    top_score = jnp.max(jnp.where(valid, scores, -1e30), axis=2, keepdims=True)
    expo = jnp.where(valid, jnp.exp(scores - top_score), 0.0)
    probs = (expo / jnp.sum(expo, axis=2, keepdims=True)).astype(jnp.bfloat16)
    context = jnp.einsum(
        "rht,rtc->rhc", probs, cache[:, :, :latent_size], preferred_element_type=jnp.float32
    ).astype(jnp.bfloat16)
    by_head = lax.all_to_all(context, ("ep", "side"), split_axis=1, concat_axis=0, tiled=True)
    values = jnp.einsum(
        "rhc,hcd->rhd", by_head, uv_weight, preferred_element_type=jnp.float32
    ).astype(jnp.bfloat16)
    attn = lax.psum_scatter(
        jnp.dot(
            values.reshape(lax.axis_size(("ep", "side")) * rows_here, heads_here * value_size),
            out_weight,
            preferred_element_type=jnp.float32,
        ),
        ("ep", "side"),
        scatter_dimension=0,
        tiled=True,
    )
    wide = resid.astype(jnp.float32) + attn
    hidden_state = wide.astype(jnp.bfloat16)
    wide = hidden_state.astype(jnp.float32)
    normed = (
        wide
        * lax.rsqrt(jnp.mean(wide * wide, axis=1, keepdims=True) + 1e-06)
        * norm_gain.astype(jnp.float32)
    ).astype(jnp.bfloat16)
    expert_count = lax.axis_size("ep")
    side_count = lax.axis_size("side")
    experts_range = jnp.arange(expert_count, dtype=jnp.int32)
    chosen = expert_ids[:, :, None] == experts_range[None, None, :]
    coef = jnp.sum(route_weights[:, :, None] * chosen.astype(jnp.float32), axis=1)
    named = jnp.any(chosen, axis=1)
    buckets = jnp.where(named.T[:, :, None], normed[None, :, :], jnp.zeros((), jnp.bfloat16))
    width = normed.shape[1]
    copies = jnp.broadcast_to(buckets[:, None], (expert_count, side_count, rows_here, width))
    copies = copies.reshape(expert_count * side_count, rows_here, width)
    arrived = lax.all_to_all(copies, ("ep", "side"), split_axis=0, concat_axis=1, tiled=True)
    gate = jnp.dot(arrived[0], gate_weight[0], preferred_element_type=jnp.float32)
    upper = jnp.dot(arrived[0], up_weight[0], preferred_element_type=jnp.float32)
    inner = (jax.nn.silu(gate) * upper).astype(jnp.bfloat16)
    partial_out = jnp.dot(inner, down_weight[0], preferred_element_type=jnp.float32)[None]
    returned = lax.all_to_all(
        partial_out.astype(jnp.bfloat16), ("ep", "side"), split_axis=1, concat_axis=0, tiled=True
    ).astype(partial_out.dtype)
    expert_out = jnp.sum(
        returned.reshape(expert_count, side_count, rows_here, width), axis=1
    ).astype(jnp.bfloat16)
    mixed = jnp.einsum("re,erd->rd", coef, expert_out.astype(jnp.float32))
    return (wide + mixed).astype(jnp.bfloat16)


def solution(mesh):
    return jax.shard_map(
        on_device,
        mesh=mesh,
        in_specs=(
            P(("group", "ep", "side"), None, None),
            P(("group", "ep", "side"), None, None),
            P(("group", "ep", "side")),
            P(("group", "ep", "side"), None),
            P(("ep", "side"), None, None),
            P(("ep", "side"), None),
            P(),
            P(("group", "ep", "side"), None),
            P(("group", "ep", "side"), None),
            P("ep", None, "side"),
            P("ep", None, "side"),
            P("ep", "side", None),
        ),
        out_specs=P(("group", "ep", "side"), None),
        check_vma=False,
    )
```

profile of v0, /device:TPU:0, one launch (start us, length us, event | category | flops | bytes accessed | tf_op | source)
XLA Modules:
  0.0 196.6 jit_solution(16103546774003448570)
XLA Ops:
  6.5 0.0 copy-start
  6.5 0.0 all-reduce.3.cloned.1.call-start
  6.5 0.8 iota_compare_fusion.1
  7.4 1.5 convolution_multiply_fusion
  8.8 0.2 fusion.52
  9.0 1.6 convolution_convert_fusion.1
  10.6 0.3 copy.33
  10.9 17.2 %all_to_all.39 = bf16[2,128,512]{2,0,1:T(2,128)(2,1)S(1)} all-to-all(bf16[2,128,512]{2,0,1:T(2,128)(2,1)S(1)} %copy.33), channel_id=1, replica_groups=mesh['group'=2,'ep'=4,'side'=4] {'ep','side'}, dimensions={1} | all-to-all | bytes 524288 | tf_op jit(solution)/shard_map/all_to_all | solution.py:36
  28.2 0.2 copy.53
  28.3 0.1 all_to_all.32
  28.5 0.0 copy-done
  28.5 0.3 fusion.10
  28.7 0.0 copy-start.2
  28.7 0.0 copy-start.4
  28.8 0.0 copy-start.5
  28.8 0.0 copy-start.1
  28.8 8.8 %fusion.26 = f32[32,7168]{1,0:T(8,128)} fusion(bf16[1024,7168]{1,0:T(8,128)(2,1)} %param.17, bf16[8,4,8,128]{3,2,1,0:T(8,128)(2,1)S(1)} %fusion.10), kind=kOutput, calls=%fused_computation.31 | convolution fusion | flops 469762048 | bytes 15663104 | tf_op jit(solution)/shard_map/dot_general | solution.py:41
  37.6 0.0 all-reduce.3.cloned.1.call-update
  37.7 0.0 copy-done.2
  37.7 0.0 copy-done.4
  37.7 0.1 fusion.44
  37.8 0.1 copy.36
  37.9 0.0 copy-done.5
  37.9 0.6 dynamic-slice
  39.1 89.4 %all-reduce.3.cloned.1.call-done = f32[32,7168]{1,0:T(8,128)} async-done(((f32[32,7168]{1,0:T(8,128)}), f32[32,7168]{1,0:T(8,128)}) %all-reduce.3.cloned.1.call-update) | async-done | bytes 917520
  128.5 0.0 copy-done.1
  128.5 1.1 fusion.34
  129.7 0.1 fusion.36
  129.8 0.2 broadcast_select_fusion
  129.9 0.2 broadcast_in_dim.62
  130.2 19.2 %all_to_all.40 = bf16[16,2,7168]{2,1,0:T(2,128)(2,1)S(1)} all-to-all(bf16[16,2,7168]{2,1,0:T(2,128)(2,1)S(1)} %bitcast.51), channel_id=1, replica_groups=mesh['group'=2,'ep'=4,'side'=4] {'ep','side'}, dimensions={0} | all-to-all | bytes 917504 | tf_op jit(solution)/shard_map/all_to_all | solution.py:68
  149.3 0.2 squeeze.13
  149.5 4.4 %fusion.5 = f32[32,512]{1,0:T(8,128)S(1)} fusion(bf16[32,7168]{1,0:T(8,128)(2,1)S(1)} %squeeze.13, bf16[1,7168,512]{2,1,0:T(8,128)(2,1)} %param.21), kind=kOutput, calls=%fused_computation.6 | convolution fusion | flops 234881024 | bytes 7864320 | tf_op jit(solution)/shard_map/dot_general | solution.py:69
  153.9 0.0 copy-start.3
  153.9 7.9 %fusion.1 = bf16[1,32,7168]{2,1,0:T(8,128)(2,1)S(1)} fusion(bf16[1,512,7168]{2,1,0:T(8,128)(2,1)} %param.23, bf16[32,7168]{1,0:T(8,128)(2,1)S(1)} %squeeze.13, bf16[1,7168,512]{2,1,0:T(8,128)(2,1)} %param.22, f32[32,512]{1,0:T(8,128)S(1)} %fusion.5), kind=kOutput, calls=%fused_computation.2 | convolution fusion | flops 470089728 | bytes 15663104 | tf_op jit(solution)/shard_map/dot_general | solution.py:72
  161.8 0.7 copy.54
  162.6 0.5 broadcast.61
  163.1 3.4 %reduce.3 = bf16[32,7168]{1,0:T(8,128)(2,1)S(1)} reduce(bf16[32,1,7168]{2,1,0:T(2,128)(2,1)S(1)} %bitcast.50, bf16[]{:T(256)} %broadcast.61), dimensions={1}, to_apply=%bitcast.49.reduce_sub_computation | reduce | bytes 917506
  166.4 0.9 reshape.60
  167.4 3.7 %all-to-all-start.2 = ((bf16[16,2,7168]{2,1,0:T(2,128)(2,1)}), bf16[16,2,7168]{2,1,0:T(2,128)(2,1)S(1)}, u32[]{:S(2)}, u32[]{:S(2)}) async-start(bf16[16,2,7168]{2,1,0:T(2,128)(2,1)} %reshape.60), calls=%async_computation.2 | async-start | bytes 917504 | tf_op jit(solution)/shard_map/all_to_all | solution.py:73
  171.1 0.0 copy-done.3
  171.2 0.1 select_reduce_fusion.1
  171.2 14.0 %all-to-all-done.2 = bf16[16,2,7168]{2,1,0:T(2,128)(2,1)S(1)} async-done(((bf16[16,2,7168]{2,1,0:T(2,128)(2,1)}), bf16[16,2,7168]{2,1,0:T(2,128)(2,1)S(1)}, u32[]{:S(2)}, u32[]{:S(2)}) %all-to-all-start.2) | async-done | bytes 458784 | tf_op jit(solution)/shard_map/all_to_all | solution.py:73
  185.2 0.4 reshape.61
  185.6 2.6 %bitcast_reduce_fusion = bf16[32,7168]{1,0:T(8,128)(2,1)S(1)} fusion(bf16[32,1,7168]{2,1,0:T(2,128)(2,1)S(1)} %reshape.61), kind=kLoop, calls=%fused_computation.57 | loop fusion | bytes 917504 | tf_op jit(solution)/shard_map/all_to_all | solution.py:73
  188.2 0.2 all_to_all.35
  188.4 0.6 reduce_sum.42
  188.9 0.2 fusion.24
  189.1 0.7 fusion.37
  (2 shorter events, 0.0 us)
Async XLA Ops:
  6.5 21.9 %copy-start = (bf16[8,512,128]{2,1,0:T(8,128)(2,1)S(1)}, bf16[8,512,128]{2,1,0:T(8,128)(2,1)}, u32[]{:S(2)}) copy-start(bf16[8,512,128]{2,1,0:T(8,128)(2,1)} %param.16) | copy-start | bytes 3145732
  6.5 122.0 %all-reduce.3.cloned.1.call-start = ((), (), s32[]{:S(2)}) async-start(), calls=%async_computation.3 | async-start | bytes 1835008
  28.7 8.9 %copy-start.2 = (bf16[7168]{0:T(1024)(128)(2,1)S(1)}, bf16[7168]{0:T(1024)(128)(2,1)}, u32[]{:S(2)}) copy-start(bf16[7168]{0:T(1024)(128)(2,1)} %param.18) | copy-start | bytes 43012
  28.7 8.9 %copy-start.4 = (s32[2,2]{1,0:T(2,128)S(1)}, s32[2,2]{1,0:T(2,128)}, u32[]{:S(2)}) copy-start(s32[2,2]{1,0:T(2,128)} %param.19) | copy-start | bytes 52
  28.8 9.1 %copy-start.5 = (u32[32]{0:T(128)S(1)}, u32[32]{0:T(128)}, u32[]{:S(2)}) copy-start(u32[32]{0:T(128)} %constant.34) | copy-start | bytes 388
  28.8 99.8 %copy-start.1 = (bf16[2,7168]{1,0:T(2,128)(2,1)S(1)}, bf16[2,7168]{1,0:T(2,128)(2,1)}, u32[]{:S(2)}) copy-start(bf16[2,7168]{1,0:T(2,128)(2,1)} %param.15) | copy-start | bytes 86020
  153.9 17.2 %copy-start.3 = (f32[2,2]{1,0:T(2,128)S(1)}, f32[2,2]{1,0:T(2,128)}, u32[]{:S(2)}) copy-start(f32[2,2]{1,0:T(2,128)} %param.20) | copy-start | bytes 52
  167.4 17.8 %all-to-all-start.2 = ((bf16[16,2,7168]{2,1,0:T(2,128)(2,1)}), bf16[16,2,7168]{2,1,0:T(2,128)(2,1)S(1)}, u32[]{:S(2)}, u32[]{:S(2)}) async-start(bf16[16,2,7168]{2,1,0:T(2,128)(2,1)} %reshape.60), calls=%async_computation.2 | async-start | bytes 917504 | tf_op jit(solution)/shard_map/all_to_all | solution.py:73
Sparse Core Ops, SparseCore 0:
  37.8 90.7 all-reduce.2
where the time goes:
time: 197 us
  waiting for transfers between devices  103 us (52%)
  blocking collectives  36.4 us (18%)
  matrix products  24.7 us (13%)
  between operations  14.2 us (7%)
  other arithmetic  7.18 us (4%)
  local copies, waits for them, and re-layouts  7.01 us (4%)
  starting transfers between devices  3.74 us (2%)
    unnamed x2, waiting for transfers between devices  89.4 us
    all_to_all x1, blocking collectives, on_device(): lax.all_to_all(copies, ('ep', 'side'), split_axis=0, concat_axis=1, tiled...  19.2 us
    all_to_all x1, blocking collectives, on_device(): lax.all_to_all(context, ('ep', 'side'), split_axis=1, concat_axis=0, tile...  17.2 us
    all_to_all x1, waiting for transfers between devices, on_device(): lax.all_to_all(partial_out.astype(jnp.bfloat16), ('ep', 'side'), split_ax...  14 us
    dot_general x1, matrix products, on_device(): jnp.dot(values.reshape(lax.axis_size(('ep', 'side')) * rows_here, heads_h...  8.84 us
    dot_general x1, matrix products, on_device(): jnp.dot(inner, down_weight[0], preferred_element_type=jnp.float32)[None]  7.89 us
    dot_general x1, matrix products, on_device(): jnp.dot(arrived[0], gate_weight[0], preferred_element_type=jnp.float32)  4.42 us
  transfers between devices with their start and end apart: 2, of which 2 were waited for; matrix products, arithmetic and copies ran while one was open for 0% of the time, Pallas kernels for 0%

commit v1 on v0

v1 whole, which is shorter than its diff:
```python
import functools

import jax
import jax.numpy as jnp
from jax import lax
from jax.experimental import pallas as pl
from jax.experimental.pallas import tpu as pltpu
from jax.sharding import PartitionSpec as P

F32 = jnp.float32
BF16 = jnp.bfloat16
MESH = pl.DeviceIdType.MESH
CHUNKS = 4


def layer_kernel(
    ep_n,
    side_n,
    lengths,
    ids,
    route,
    q_hbm,
    cache_hbm,
    resid,
    gain,
    uv_hbm,
    ow_hbm,
    gw_hbm,
    uw_hbm,
    dw_hbm,
    out,
    q,
    cache,
    uv,
    ow,
    gw,
    uw,
    dw,
    ctx_tx,
    ctx_rx,
    ctx_rows,
    vals,
    cf_tx,
    cf_rx,
    cf_rows,
    part,
    t1,
    r1,
    t2,
    r2,
    t3,
    r3,
    keep,
    hidden,
    gath,
    xrows,
    in_sem,
    ow_sem,
    gw_sem,
    uw_sem,
    dw_sem,
    ctx_send,
    ctx_recv,
    cf_send,
    cf_recv,
    rs_send,
    rs_recv,
    ag_send,
    ag_recv,
):
    n = ep_n * side_n
    x_n = ep_n // 2
    ep = lax.axis_index("ep")
    side = lax.axis_index("side")
    me = ep * side_n + side
    x = ep // 2
    core = lax.rem(ep, 2)
    rows_here, heads, _ = q_hbm.shape
    heads_here, latent, value_size = uv_hbm.shape
    slots = cache_hbm.shape[1]
    width = resid.shape[1]
    piece = width // CHUNKS
    rows = n * rows_here
    block = side_n * rows_here

    def at(group_index):
        return {"ep": group_index // side_n, "side": lax.rem(group_index, side_n)}

    def remote(src, dst, send, recv, device):
        return pltpu.make_async_remote_copy(
            src_ref=src, dst_ref=dst, send_sem=send, recv_sem=recv, device_id=device, device_id_type=MESH
        )

    barrier = pltpu.get_barrier_semaphore()

    @pl.loop(1, n)
    def _(i):
        pl.semaphore_signal(barrier, inc=1, device_id=at(lax.rem(me + i, n)), device_id_type=MESH)

    loads = [
        pltpu.make_async_copy(cache_hbm, cache, in_sem.at[0]),
        pltpu.make_async_copy(q_hbm, q, in_sem.at[1]),
        pltpu.make_async_copy(uv_hbm, uv, in_sem.at[2]),
    ]
    for load in loads:
        load.start()
    cut = [pl.ds(c * piece, piece) for c in range(CHUNKS)]
    ow_load = [pltpu.make_async_copy(ow_hbm.at[:, s], ow.at[:, s], ow_sem.at[c]) for c, s in enumerate(cut)]
    gw_load = [pltpu.make_async_copy(gw_hbm.at[0, s], gw.at[s], gw_sem.at[c]) for c, s in enumerate(cut)]
    uw_load = [pltpu.make_async_copy(uw_hbm.at[0, s], uw.at[s], uw_sem.at[c]) for c, s in enumerate(cut)]
    dw_load = [pltpu.make_async_copy(dw_hbm.at[0, :, s], dw.at[:, s], dw_sem.at[c]) for c, s in enumerate(cut)]
    for load in ow_load:
        load.start()
    for c in range(CHUNKS):
        gw_load[c].start()
        uw_load[c].start()
    for load in dw_load:
        load.start()

    lane = lax.broadcasted_iota(jnp.int32, (1, 128), 1)
    for r in range(rows_here):
        line = jnp.zeros((1, 128), F32)
        for k in range(ids.shape[1]):
            line += jnp.where(lane == ids[r, k], route[r, k], 0.0)
        cf_tx[r : r + 1, :] = line
    cf_rx[me] = cf_tx[...]

    def attend(r):
        scores = lax.dot_general(
            q[r], cache[r], (((1,), (1,)), ((), ())), preferred_element_type=F32
        ) * (1.0 / 192.0**0.5)
        valid = lax.broadcasted_iota(jnp.int32, (heads, slots), 1) < lengths[r]
        top = jnp.max(jnp.where(valid, scores, -1e30), axis=1, keepdims=True)
        expo = jnp.where(valid, jnp.exp(scores - top), 0.0)
        probs = (expo / jnp.sum(expo, axis=1, keepdims=True)).astype(BF16)
        context = jnp.dot(probs, cache[r, :, :latent], preferred_element_type=F32)
        for d in range(n):
            ctx_tx[r, d] = context[d * heads_here : (d + 1) * heads_here].astype(BF16)
        ctx_rx[r, me] = ctx_tx[r, me]

    def send_context(r):
        @pl.loop(1, n)
        def _(i):
            there = lax.rem(me + i, n)
            remote(
                ctx_tx.at[r, there], ctx_rx.at[r, me], ctx_send.at[r, i - 1], ctx_recv.at[r, i - 1], at(there)
            ).start()

    loads[0].wait()
    loads[1].wait()
    for r in range(rows_here):
        attend(r)
        if r == 0:
            pl.semaphore_wait(barrier, n - 1)
        send_context(r)

    @pl.loop(1, n)
    def _(i):
        remote(cf_tx, cf_rx.at[me], cf_send.at[i - 1], cf_recv.at[i - 1], at(lax.rem(me + i, n))).start()

    loads[2].wait()
    for r in range(rows_here):

        @pl.loop(1, n)
        def _(i):
            origin = lax.rem(me + n - i, n)
            remote(
                ctx_tx.at[r, origin], ctx_rx.at[r, origin], ctx_send.at[r, i - 1], ctx_recv.at[r, i - 1], at(origin)
            ).wait_recv()

    for r in range(rows_here):
        for d in range(n):
            first = (d * rows_here + r) * heads_here
            arrived = ctx_rx[r, d].astype(F32)
            for j in range(latent // 128):
                ctx_rows[j, first : first + heads_here] = arrived[:, j * 128 : (j + 1) * 128]
    for h in range(heads_here):
        picked = pl.ds(h, rows, stride=heads_here) if heads_here > 1 else pl.ds(0, rows)
        taken = jnp.concatenate([ctx_rows[j, picked, :] for j in range(latent // 128)], axis=1)
        vals[:, h * value_size : (h + 1) * value_size] = jnp.dot(
            taken.astype(BF16), uv[h], preferred_element_type=F32
        ).astype(BF16)

    def reduce_copies(p, c):
        core_copy = remote(
            t1.at[p, c], r1.at[p, c], rs_send.at[p, c, 0], rs_recv.at[p, c, 0], {"ep": ep + 1 - 2 * core}
        )
        x_copies, side_copies = [], []
        for i in range(1, x_n):
            there = lax.rem(x + i, x_n) * 2 + core
            x_copies.append(
                remote(t2.at[p, c, i - 1], r2.at[p, c, i - 1], rs_send.at[p, c, i], rs_recv.at[p, c, i], {"ep": there})
            )
        for i in range(1, side_n):
            k = x_n + i - 1
            there = lax.rem(side + i, side_n)
            side_copies.append(
                remote(t3.at[p, c, there], r3.at[p, c, i - 1], rs_send.at[p, c, k], rs_recv.at[p, c, k], {"side": there})
            )
        return core_copy, x_copies, side_copies

    def reduce_scatter(p, product):
        copies = [reduce_copies(p, c) for c in range(CHUNKS)]
        totals = []
        for step in range(CHUNKS + 2):
            c = step
            if c < CHUNKS:
                part[c] = product(c).reshape(ep_n, block, piece)
                for k in range(x_n):
                    t1[p, c, k] = part[c, 2 * k + 1 - core].astype(BF16)
                copies[c][0].start()
            c = step - 1
            if 0 <= c < CHUNKS:
                copies[c][0].wait_recv()
                for i in range(1, x_n):
                    k = lax.rem(x + i, x_n)
                    t2[p, c, i - 1] = (part[c, 2 * k + core] + r1[p, c, k].astype(F32)).astype(BF16)
                    copies[c][1][i - 1].start()
            c = step - 2
            if 0 <= c < CHUNKS:
                total = part[c, ep] + r1[p, c, x].astype(F32)
                for i in range(1, x_n):
                    copies[c][1][i - 1].wait_recv()
                    total += r2[p, c, i - 1].astype(F32)
                for s in range(side_n):
                    mine = total[s * rows_here : (s + 1) * rows_here]
                    keep[c, s] = mine
                    t3[p, c, s] = mine.astype(BF16)
                for copy in copies[c][2]:
                    copy.start()
        for c in range(CHUNKS):
            total = keep[c, side]
            for i in range(1, side_n):
                copies[c][2][i - 1].wait_recv()
                total += r3[p, c, i - 1].astype(F32)
            totals.append(total)
        return totals, copies

    def out_product(c):
        ow_load[c].wait()
        return jnp.dot(vals[...], ow[:, cut[c]], preferred_element_type=F32)

    attn, copies_a = reduce_scatter(0, out_product)

    square = jnp.zeros((rows_here, 1), F32)
    for c in range(CHUNKS):
        state = (resid[:, cut[c]].astype(F32) + attn[c]).astype(BF16).astype(F32)
        hidden[:, cut[c]] = state
        square += jnp.sum(state * state, axis=1, keepdims=True)
    inverse = lax.rsqrt(square * (1.0 / width) + 1e-06)

    def gather_copies(c):
        def blocks(index):
            return gath.at[c, pl.ds(index * side_n, side_n)]

        side_out, side_in, x_out, x_in, core_out, core_in = [], [], [], [], [], []
        for i in range(1, side_n):
            k = i - 1
            origin = ep * side_n + lax.rem(side + side_n - i, side_n)
            there = {"side": lax.rem(side + i, side_n)}
            side_out.append(remote(gath.at[c, me], gath.at[c, me], ag_send.at[c, k], ag_recv.at[c, k], there))
            side_in.append(remote(gath.at[c, origin], gath.at[c, origin], ag_send.at[c, k], ag_recv.at[c, k], there))
        for i in range(1, x_n):
            k = side_n + i - 2
            origin = lax.rem(x + x_n - i, x_n) * 2 + core
            there = {"ep": lax.rem(x + i, x_n) * 2 + core}
            x_out.append(remote(blocks(ep), blocks(ep), ag_send.at[c, k], ag_recv.at[c, k], there))
            x_in.append(remote(blocks(origin), blocks(origin), ag_send.at[c, k], ag_recv.at[c, k], there))
        for i in range(x_n):
            k = side_n + x_n - 2 + i
            origin = lax.rem(x + x_n - i, x_n) * 2
            sibling = {"ep": ep + 1 - 2 * core}
            mine, other = blocks(origin + core), blocks(origin + 1 - core)
            core_out.append(remote(mine, mine, ag_send.at[c, k], ag_recv.at[c, k], sibling))
            core_in.append(remote(other, other, ag_send.at[c, k], ag_recv.at[c, k], sibling))
        return side_out, side_in, x_out, x_in, core_out, core_in

    gathers = [gather_copies(c) for c in range(CHUNKS)]
    for c in range(CHUNKS):
        gath[c, me] = (hidden[:, cut[c]] * inverse * gain[:, cut[c]].astype(F32)).astype(BF16)
        for copy in gathers[c][0]:
            copy.start()
    for c in range(CHUNKS):
        for copy in gathers[c][1]:
            copy.wait_recv()
        for copy in gathers[c][2]:
            copy.start()
        gathers[c][4][0].start()
    for c in range(CHUNKS):
        for i in range(1, x_n):
            gathers[c][3][i - 1].wait_recv()
            gathers[c][4][i].start()

    @pl.loop(1, n)
    def _(i):
        origin = lax.rem(me + n - i, n)
        remote(cf_tx, cf_rx.at[origin], cf_send.at[i - 1], cf_recv.at[i - 1], at(origin)).wait_recv()

    for d in range(n):
        cf_rows[d * rows_here : (d + 1) * rows_here] = cf_rx[d]
    coef = jnp.sum(jnp.where(lane == ep, cf_rows[...], 0.0), axis=1, keepdims=True)

    gate = jnp.zeros((rows, gw.shape[1]), F32)
    upper = jnp.zeros((rows, gw.shape[1]), F32)
    for c in range(CHUNKS):
        for copy in gathers[c][5]:
            copy.wait_recv()
        for d in range(n):
            xrows[c, d * rows_here : (d + 1) * rows_here] = gath[c, d].astype(F32)
        normed = xrows[c].astype(BF16)
        gw_load[c].wait()
        uw_load[c].wait()
        gate += jnp.dot(normed, gw[cut[c]], preferred_element_type=F32)
        upper += jnp.dot(normed, uw[cut[c]], preferred_element_type=F32)
    inner = (jax.nn.silu(gate) * upper * coef).astype(BF16)

    def down_product(c):
        dw_load[c].wait()
        return jnp.dot(inner, dw[:, cut[c]], preferred_element_type=F32)

    mixed, copies_b = reduce_scatter(1, down_product)
    for c in range(CHUNKS):
        out[:, cut[c]] = (hidden[:, cut[c]] + mixed[c]).astype(out.dtype)

    @pl.loop(1, n)
    def _(i):
        there = lax.rem(me + i, n)
        for r in range(rows_here):
            remote(
                ctx_tx.at[r, there], ctx_rx.at[r, me], ctx_send.at[r, i - 1], ctx_recv.at[r, i - 1], at(there)
            ).wait_send()
        remote(cf_tx, cf_rx.at[me], cf_send.at[i - 1], cf_recv.at[i - 1], at(there)).wait_send()

    for copies in (copies_a, copies_b):
        for core_copy, x_copies, side_copies in copies:
            for copy in [core_copy] + x_copies + side_copies:
                copy.wait_send()
    for side_out, _, x_out, _, core_out, _ in gathers:
        for copy in side_out + x_out + core_out:
            copy.wait_send()


def on_device(
    queries,
    cache,
    lengths,
    resid,
    uv_weight,
    out_weight,
    norm_gain,
    expert_ids,
    route_weights,
    gate_weight,
    up_weight,
    down_weight,
):
    ep_n = lax.axis_size("ep")
    side_n = lax.axis_size("side")
    n = ep_n * side_n
    x_n = ep_n // 2
    rows_here, _, _ = queries.shape
    heads_here, latent, value_size = uv_weight.shape
    width = resid.shape[1]
    piece = width // CHUNKS
    rows = n * rows_here
    block = side_n * rows_here
    vmem = pltpu.VMEM
    dma = pltpu.SemaphoreType.DMA
    hops = 1 + (x_n - 1) + (side_n - 1)
    gather_hops = (side_n - 1) + (x_n - 1) + x_n
    smem_spec = pl.BlockSpec(memory_space=pltpu.SMEM)
    vmem_spec = pl.BlockSpec(memory_space=pltpu.VMEM)
    any_spec = pl.BlockSpec(memory_space=pl.ANY)
    return pl.pallas_call(
        functools.partial(layer_kernel, ep_n, side_n),
        out_shape=jax.ShapeDtypeStruct(resid.shape, resid.dtype),
        in_specs=[smem_spec] * 3 + [any_spec] * 2 + [vmem_spec] * 2 + [any_spec] * 5,
        out_specs=vmem_spec,
        scratch_shapes=[
            vmem(queries.shape, BF16),
            vmem(cache.shape, BF16),
            vmem(uv_weight.shape, BF16),
            vmem(out_weight.shape, BF16),
            vmem(gate_weight.shape[1:], BF16),
            vmem(up_weight.shape[1:], BF16),
            vmem(down_weight.shape[1:], BF16),
            vmem((rows_here, n, heads_here, latent), BF16),
            vmem((rows_here, n, heads_here, latent), BF16),
            vmem((latent // 128, rows * heads_here, 128), F32),
            vmem((rows, heads_here * value_size), BF16),
            vmem((rows_here, 128), F32),
            vmem((n, rows_here, 128), F32),
            vmem((rows, 128), F32),
            vmem((CHUNKS, ep_n, block, piece), F32),
            vmem((2, CHUNKS, x_n, block, piece), BF16),
            vmem((2, CHUNKS, x_n, block, piece), BF16),
            vmem((2, CHUNKS, x_n - 1, block, piece), BF16),
            vmem((2, CHUNKS, x_n - 1, block, piece), BF16),
            vmem((2, CHUNKS, side_n, rows_here, piece), BF16),
            vmem((2, CHUNKS, side_n - 1, rows_here, piece), BF16),
            vmem((CHUNKS, side_n, rows_here, piece), F32),
            vmem((rows_here, width), F32),
            vmem((CHUNKS, n, rows_here, piece), BF16),
            vmem((CHUNKS, rows, piece), F32),
            dma((3,)),
            dma((CHUNKS,)),
            dma((CHUNKS,)),
            dma((CHUNKS,)),
            dma((CHUNKS,)),
            dma((rows_here, n - 1)),
            dma((rows_here, n - 1)),
            dma((n - 1,)),
            dma((n - 1,)),
            dma((2, CHUNKS, hops)),
            dma((2, CHUNKS, hops)),
            dma((CHUNKS, gather_hops)),
            dma((CHUNKS, gather_hops)),
        ],
        compiler_params=pltpu.CompilerParams(
            collective_id=0, has_side_effects=True, vmem_limit_bytes=56 * 2**20
        ),
    )(
        lengths,
        expert_ids,
        route_weights,
        queries,
        cache,
        resid,
        norm_gain.reshape(1, width),
        uv_weight,
        out_weight,
        gate_weight,
        up_weight,
        down_weight,
    )


def solution(mesh):
    return jax.shard_map(
        on_device,
        mesh=mesh,
        in_specs=(
            P(("group", "ep", "side"), None, None),
            P(("group", "ep", "side"), None, None),
            P(("group", "ep", "side")),
            P(("group", "ep", "side"), None),
            P(("ep", "side"), None, None),
            P(("ep", "side"), None),
            P(),
            P(("group", "ep", "side"), None),
            P(("group", "ep", "side"), None),
            P("ep", None, "side"),
            P("ep", None, "side"),
            P("ep", "side", None),
        ),
        out_specs=P(("group", "ep", "side"), None),
        check_vma=False,
    )
```

time: 197 us -> 64.3 us (0.33)
  waiting for transfers between devices: 103 us -> 0 us
  Pallas kernels: 0 us -> 57.2 us
  blocking collectives: 36.4 us -> 0 us
  matrix products: 24.7 us -> 0 us
  between operations: 14.2 us -> 0.01 us
  other arithmetic: 7.18 us -> 0 us
  starting transfers between devices: 3.74 us -> 0 us
    unnamed x2 -> x0, waiting for transfers between devices: 89.4 us -> none
    pallas_call x0 -> x1, Pallas kernels: none -> 57.2 us  [on_device(): pl.pallas_call(functools.partial(layer_kernel, ep_n, side_n), out_shape=j...]
    all_to_all x2 -> x0, blocking collectives: 36.4 us -> none  [the longest x1 19.2 us: on_device(): lax.all_to_all(copies, ('ep', 'side'), split_axis=0, concat_axis=1, tiled...]
    dot_general x7 -> x0, matrix products: 24.7 us -> none  [the longest x1 8.84 us: on_device(): jnp.dot(values.reshape(lax.axis_size(('ep', 'side')) * rows_here, heads_h...]
    all_to_all x1 -> x0, waiting for transfers between devices: 14 us -> none  [on_device(): lax.all_to_all(partial_out.astype(jnp.bfloat16), ('ep', 'side'), split_ax...]
    all_to_all x1 -> x0, starting transfers between devices: 3.74 us -> none  [on_device(): lax.all_to_all(partial_out.astype(jnp.bfloat16), ('ep', 'side'), split_ax...]
    unnamed x1 -> x0, other arithmetic: 3.37 us -> none
    all_to_all x4 -> x0, local copies, waits for them, and re-layouts: 3.06 us -> none  [the longest x2 2.78 us: on_device(): lax.all_to_all(partial_out.astype(jnp.bfloat16), ('ep', 'side'), split_ax...]
  transfers between devices with their start and end apart: 2 -> 0, of which waited for: 2 -> 0; matrix products, arithmetic and copies ran while one was open for 0% -> 0% of each run, Pallas kernels for 0% -> 0%
where the time goes in v1:
time: 64.3 us; the launch traced here: 63.9 us
  Pallas kernels  57.2 us (89%)
  local copies, waits for them, and re-layouts  6.71 us (10%)
    pallas_call x1, Pallas kernels, on_device(): pl.pallas_call(functools.partial(layer_kernel, ep_n, side_n), out_shape=j...  57.2 us
    unnamed x3, local copies, waits for them, and re-layouts  5.38 us
    reshape x1, local copies, waits for them, and re-layouts, on_device(): norm_gain.reshape(1, width)  1.34 us

profile of v1, /device:TPU:0, one launch (start us, length us, event | category | flops | bytes accessed | tf_op | source)
XLA Modules:
  0.0 63.9 jit_solution(8422446087290115660)
XLA Ops:
  0.0 1.3 %reshape.3.gain = bf16[1,7168]{1,0:T(2,128)(2,1)} reshape(bf16[7168]{0:T(1024)(128)(2,1)} %param.18) | data formatting | bytes 28672 | tf_op jit(solution)/shard_map/reshape | solution.py:429
  1.3 1.9 %copy.13.q_hbm = bf16[2,128,576]{2,1,0:T(8,128)(2,1)} copy(bf16[2,128,576]{1,2,0:T(8,128)(2,1)} %param.12) | data formatting | bytes 589824 | tf_op args[0]
  3.2 2.1 %copy.14.cache_hbm = bf16[2,256,576]{2,1,0:T(8,128)(2,1)} copy(bf16[2,256,576]{1,2,0:T(8,128)(2,1)} %param.13) | data formatting | bytes 1179648 | tf_op args[1]
  5.3 57.2 %shard_map.118 = bf16[2,7168]{1,0:T(2,128)(2,1)} custom-call(s32[2]{0:T(128)} %lengths.1, s32[2,2]{1,0:T(2,128)} %ids.1, f32[2,2]{1,0:T(2,128)} %route.1, bf16[2,128,576]{2,1,0:T(8,128)(2,1)} %copy.13.q_hbm, bf16[2,256,576]{2,1,0:T(8,128)(2,1)} %copy.14.cache_hbm, bf16[2,7168]{1,0:T(2,128)(2,1)} %resid.1, bf16[1,7168]{1,0:T(2,128)(2,1)} %reshape.3.gain, ...), custom_call_target="tpu_custom_call" | custom-call | tf_op jit(solution)/shard_map/pallas_call | solution.py:374
  62.5 1.4 %copy.16 = bf16[2,7168]{1,0:T(2,128)(2,1)} copy(bf16[2,7168]{1,0:T(2,128)(2,1)} %shard_map.118) | data formatting | bytes 57344

commit v2 on v1

--- a/solution.py
+++ b/solution.py
@@ -10,7 +10,7 @@
 F32 = jnp.float32
 BF16 = jnp.bfloat16
 MESH = pl.DeviceIdType.MESH
-CHUNKS = 4
+CHUNKS = 2
 
 
 def layer_kernel(
@@ -75,9 +75,9 @@
     me = ep * side_n + side
     x = ep // 2
     core = lax.rem(ep, 2)
-    rows_here, heads, _ = q_hbm.shape
+    rows_here, _, heads = q_hbm.shape
     heads_here, latent, value_size = uv_hbm.shape
-    slots = cache_hbm.shape[1]
+    slots = cache_hbm.shape[2]
     width = resid.shape[1]
     piece = width // CHUNKS
     rows = n * rows_here
@@ -111,11 +111,6 @@
     dw_load = [pltpu.make_async_copy(dw_hbm.at[0, :, s], dw.at[:, s], dw_sem.at[c]) for c, s in enumerate(cut)]
     for load in ow_load:
         load.start()
-    for c in range(CHUNKS):
-        gw_load[c].start()
-        uw_load[c].start()
-    for load in dw_load:
-        load.start()
 
     lane = lax.broadcasted_iota(jnp.int32, (1, 128), 1)
     for r in range(rows_here):
@@ -127,13 +122,15 @@
 
     def attend(r):
         scores = lax.dot_general(
-            q[r], cache[r], (((1,), (1,)), ((), ())), preferred_element_type=F32
+            q[r], cache[r], (((0,), (0,)), ((), ())), preferred_element_type=F32
         ) * (1.0 / 192.0**0.5)
         valid = lax.broadcasted_iota(jnp.int32, (heads, slots), 1) < lengths[r]
         top = jnp.max(jnp.where(valid, scores, -1e30), axis=1, keepdims=True)
         expo = jnp.where(valid, jnp.exp(scores - top), 0.0)
         probs = (expo / jnp.sum(expo, axis=1, keepdims=True)).astype(BF16)
-        context = jnp.dot(probs, cache[r, :, :latent], preferred_element_type=F32)
+        context = lax.dot_general(
+            probs, cache[r, :latent, :], (((1,), (1,)), ((), ())), preferred_element_type=F32
+        )
         for d in range(n):
             ctx_tx[r, d] = context[d * heads_here : (d + 1) * heads_here].astype(BF16)
         ctx_rx[r, me] = ctx_tx[r, me]
@@ -167,6 +164,12 @@
             remote(
                 ctx_tx.at[r, origin], ctx_rx.at[r, origin], ctx_send.at[r, i - 1], ctx_recv.at[r, i - 1], at(origin)
             ).wait_recv()
+
+    for c in range(CHUNKS):
+        gw_load[c].start()
+        uw_load[c].start()
+    for load in dw_load:
+        load.start()
 
     for r in range(rows_here):
         for d in range(n):
@@ -188,11 +191,19 @@
         x_copies, side_copies = [], []
         for i in range(1, x_n):
             there = lax.rem(x + i, x_n) * 2 + core
-            x_copies.append(
-                remote(t2.at[p, c, i - 1], r2.at[p, c, i - 1], rs_send.at[p, c, i], rs_recv.at[p, c, i], {"ep": there})
-            )
+            for s in range(side_n):
+                k = 1 + (i - 1) * side_n + s
+                x_copies.append(
+                    remote(
+                        t2.at[p, c, i - 1, s],
+                        r2.at[p, c, i - 1, s],
+                        rs_send.at[p, c, k],
+                        rs_recv.at[p, c, k],
+                        {"ep": there},
+                    )
+                )
         for i in range(1, side_n):
-            k = x_n + i - 1
+            k = (x_n - 1) * side_n + i
             there = lax.rem(side + i, side_n)
             side_copies.append(
                 remote(t3.at[p, c, there], r3.at[p, c, i - 1], rs_send.at[p, c, k], rs_recv.at[p, c, k], {"side": there})
@@ -214,20 +225,28 @@
                 copies[c][0].wait_recv()
                 for i in range(1, x_n):
                     k = lax.rem(x + i, x_n)
-                    t2[p, c, i - 1] = (part[c, 2 * k + core] + r1[p, c, k].astype(F32)).astype(BF16)
-                    copies[c][1][i - 1].start()
+                    ahead = (part[c, 2 * k + core] + r1[p, c, k].astype(F32)).astype(BF16)
+                    for s in range(side_n):
+                        t2[p, c, i - 1, s] = ahead[s * rows_here : (s + 1) * rows_here]
+                        copies[c][1][(i - 1) * side_n + s].start()
             c = step - 2
             if 0 <= c < CHUNKS:
                 total = part[c, ep] + r1[p, c, x].astype(F32)
-                for i in range(1, x_n):
-                    copies[c][1][i - 1].wait_recv()
-                    total += r2[p, c, i - 1].astype(F32)
                 for s in range(side_n):
                     mine = total[s * rows_here : (s + 1) * rows_here]
+                    for i in range(1, x_n):
+                        copies[c][1][(i - 1) * side_n + s].wait_recv()
+                        mine += r2[p, c, i - 1, s].astype(F32)
                     keep[c, s] = mine
                     t3[p, c, s] = mine.astype(BF16)
-                for copy in copies[c][2]:
-                    copy.start()
+                    away = lax.rem(s - side + side_n, side_n)
+
+                    @pl.when(away > 0)
+                    def _():
+                        k = (x_n - 1) * side_n + away
+                        remote(
+                            t3.at[p, c, s], r3.at[p, c, away - 1], rs_send.at[p, c, k], rs_recv.at[p, c, k], {"side": s}
+                        ).start()
         for c in range(CHUNKS):
             total = keep[c, side]
             for i in range(1, side_n):
@@ -261,13 +280,16 @@
             side_out.append(remote(gath.at[c, me], gath.at[c, me], ag_send.at[c, k], ag_recv.at[c, k], there))
             side_in.append(remote(gath.at[c, origin], gath.at[c, origin], ag_send.at[c, k], ag_recv.at[c, k], there))
         for i in range(1, x_n):
-            k = side_n + i - 2
             origin = lax.rem(x + x_n - i, x_n) * 2 + core
             there = {"ep": lax.rem(x + i, x_n) * 2 + core}
-            x_out.append(remote(blocks(ep), blocks(ep), ag_send.at[c, k], ag_recv.at[c, k], there))
-            x_in.append(remote(blocks(origin), blocks(origin), ag_send.at[c, k], ag_recv.at[c, k], there))
+            for j in range(side_n):
+                k = side_n - 1 + (i - 1) * side_n + j
+                turn = lax.rem(side + side_n - j, side_n)
+                mine, other = gath.at[c, ep * side_n + turn], gath.at[c, origin * side_n + turn]
+                x_out.append(remote(mine, mine, ag_send.at[c, k], ag_recv.at[c, k], there))
+                x_in.append(remote(other, other, ag_send.at[c, k], ag_recv.at[c, k], there))
         for i in range(x_n):
-            k = side_n + x_n - 2 + i
+            k = side_n - 1 + (x_n - 1) * side_n + i
             origin = lax.rem(x + x_n - i, x_n) * 2
             sibling = {"ep": ep + 1 - 2 * core}
             mine, other = blocks(origin + core), blocks(origin + 1 - core)
@@ -276,19 +298,25 @@
         return side_out, side_in, x_out, x_in, core_out, core_in
 
     gathers = [gather_copies(c) for c in range(CHUNKS)]
-    for c in range(CHUNKS):
-        gath[c, me] = (hidden[:, cut[c]] * inverse * gain[:, cut[c]].astype(F32)).astype(BF16)
+    gains = gain[...].astype(F32)
+    for c in range(CHUNKS):
+        first = c * piece // 128
+        gain_row = jnp.concatenate([gains[first + j : first + j + 1] for j in range(piece // 128)], axis=1)
+        gath[c, me] = (hidden[:, cut[c]] * inverse * gain_row).astype(BF16)
         for copy in gathers[c][0]:
             copy.start()
-    for c in range(CHUNKS):
-        for copy in gathers[c][1]:
-            copy.wait_recv()
-        for copy in gathers[c][2]:
-            copy.start()
+        for i in range(1, x_n):
+            gathers[c][2][(i - 1) * side_n].start()
+    for c in range(CHUNKS):
+        for j in range(1, side_n):
+            gathers[c][1][j - 1].wait_recv()
+            for i in range(1, x_n):
+                gathers[c][2][(i - 1) * side_n + j].start()
         gathers[c][4][0].start()
     for c in range(CHUNKS):
         for i in range(1, x_n):
-            gathers[c][3][i - 1].wait_recv()
+            for j in range(side_n):
+                gathers[c][3][(i - 1) * side_n + j].wait_recv()
             gathers[c][4][i].start()
 
     @pl.loop(1, n)
@@ -358,7 +386,8 @@
     side_n = lax.axis_size("side")
     n = ep_n * side_n
     x_n = ep_n // 2
-    rows_here, _, _ = queries.shape
+    rows_here, head_count, component_count = queries.shape
+    slot_count = cache.shape[1]
     heads_here, latent, value_size = uv_weight.shape
     width = resid.shape[1]
     piece = width // CHUNKS
@@ -366,8 +395,8 @@
     block = side_n * rows_here
     vmem = pltpu.VMEM
     dma = pltpu.SemaphoreType.DMA
-    hops = 1 + (x_n - 1) + (side_n - 1)
-    gather_hops = (side_n - 1) + (x_n - 1) + x_n
+    hops = 1 + (x_n - 1) * side_n + (side_n - 1)
+    gather_hops = (side_n - 1) + (x_n - 1) * side_n + x_n
     smem_spec = pl.BlockSpec(memory_space=pltpu.SMEM)
     vmem_spec = pl.BlockSpec(memory_space=pltpu.VMEM)
     any_spec = pl.BlockSpec(memory_space=pl.ANY)
@@ -377,8 +406,8 @@
         in_specs=[smem_spec] * 3 + [any_spec] * 2 + [vmem_spec] * 2 + [any_spec] * 5,
         out_specs=vmem_spec,
         scratch_shapes=[
-            vmem(queries.shape, BF16),
-            vmem(cache.shape, BF16),
+            vmem((rows_here, component_count, head_count), BF16),
+            vmem((rows_here, component_count, slot_count), BF16),
             vmem(uv_weight.shape, BF16),
             vmem(out_weight.shape, BF16),
             vmem(gate_weight.shape[1:], BF16),
@@ -394,8 +423,8 @@
             vmem((CHUNKS, ep_n, block, piece), F32),
             vmem((2, CHUNKS, x_n, block, piece), BF16),
             vmem((2, CHUNKS, x_n, block, piece), BF16),
-            vmem((2, CHUNKS, x_n - 1, block, piece), BF16),
-            vmem((2, CHUNKS, x_n - 1, block, piece), BF16),
+            vmem((2, CHUNKS, x_n - 1, side_n, rows_here, piece), BF16),
+            vmem((2, CHUNKS, x_n - 1, side_n, rows_here, piece), BF16),
             vmem((2, CHUNKS, side_n, rows_here, piece), BF16),
             vmem((2, CHUNKS, side_n - 1, rows_here, piece), BF16),
             vmem((CHUNKS, side_n, rows_here, piece), F32),
@@ -423,10 +452,10 @@
         lengths,
         expert_ids,
         route_weights,
-        queries,
-        cache,
+        jnp.swapaxes(queries, 1, 2),
+        jnp.swapaxes(cache, 1, 2),
         resid,
-        norm_gain.reshape(1, width),
+        norm_gain.reshape(width // 128, 128),
         uv_weight,
         out_weight,
         gate_weight,

time: 64.3 us -> 50.4 us (0.78)
  Pallas kernels: 57.2 us -> 48.7 us
  local copies, waits for them, and re-layouts: 6.71 us -> 1.38 us
    pallas_call x1, Pallas kernels: 57.2 us -> 48.7 us  [on_device(): pl.pallas_call(functools.partial(layer_kernel, ep_n, side_n), out_shape=j...]
    unnamed x3 -> x1, local copies, waits for them, and re-layouts: 5.38 us -> 1.38 us
    reshape x1 -> x0, local copies, waits for them, and re-layouts: 1.34 us -> none  [on_device(): norm_gain.reshape(1, width)]
where the time goes in v2:
time: 50.4 us; the launch traced here: 50.1 us
  Pallas kernels  48.7 us (97%)
  local copies, waits for them, and re-layouts  1.38 us (3%)
    pallas_call x1, Pallas kernels, on_device(): pl.pallas_call(functools.partial(layer_kernel, ep_n, side_n), out_shape=j...  48.7 us
    unnamed x1, local copies, waits for them, and re-layouts  1.38 us

profile of v2, /device:TPU:0, one launch (start us, length us, event | category | flops | bytes accessed | tf_op | source)
XLA Modules:
  0.0 50.1 jit_solution(3114148171977125851)
XLA Ops:
  0.0 48.7 %shard_map.118 = bf16[2,7168]{1,0:T(2,128)(2,1)} custom-call(s32[2]{0:T(128)} %lengths.1, s32[2,2]{1,0:T(2,128)} %ids.1, f32[2,2]{1,0:T(2,128)} %route.1, bf16[2,576,128]{2,1,0:T(8,128)(2,1)} %bitcast.4, bf16[2,576,256]{2,1,0:T(8,128)(2,1)} %bitcast.3, bf16[2,7168]{1,0:T(2,128)(2,1)} %resid.1, bf16[56,128]{1,0:T(8,128)(2,1)} %bitcast.5, ...), custom_call_target="tpu_custom_call" | custom-call | tf_op jit(solution)/shard_map/pallas_call | solution.py:403
  48.8 1.4 %copy.14 = bf16[2,7168]{1,0:T(2,128)(2,1)} copy(bf16[2,7168]{1,0:T(2,128)(2,1)} %shard_map.118) | data formatting | bytes 57344

commit v3 on v2

--- a/solution.py
+++ b/solution.py
@@ -132,38 +132,33 @@
             probs, cache[r, :latent, :], (((1,), (1,)), ((), ())), preferred_element_type=F32
         )
         for d in range(n):
-            ctx_tx[r, d] = context[d * heads_here : (d + 1) * heads_here].astype(BF16)
-        ctx_rx[r, me] = ctx_tx[r, me]
-
-    def send_context(r):
-        @pl.loop(1, n)
-        def _(i):
-            there = lax.rem(me + i, n)
-            remote(
-                ctx_tx.at[r, there], ctx_rx.at[r, me], ctx_send.at[r, i - 1], ctx_recv.at[r, i - 1], at(there)
-            ).start()
+            ctx_tx[d, r] = context[d * heads_here : (d + 1) * heads_here].astype(BF16)
+        ctx_rx[me, r] = ctx_tx[me, r]
+
+    def context_copy(i, source, target, there):
+        return remote(ctx_tx.at[source], ctx_rx.at[target], ctx_send.at[i - 1], ctx_recv.at[i - 1], at(there))
 
     loads[0].wait()
     loads[1].wait()
     for r in range(rows_here):
         attend(r)
-        if r == 0:
-            pl.semaphore_wait(barrier, n - 1)
-        send_context(r)
+    pl.semaphore_wait(barrier, n - 1)
+
+    @pl.loop(1, n)
+    def _(i):
+        there = lax.rem(me + i, n)
+        context_copy(i, there, me, there).start()
 
     @pl.loop(1, n)
     def _(i):
         remote(cf_tx, cf_rx.at[me], cf_send.at[i - 1], cf_recv.at[i - 1], at(lax.rem(me + i, n))).start()
 
     loads[2].wait()
-    for r in range(rows_here):
-
-        @pl.loop(1, n)
-        def _(i):
-            origin = lax.rem(me + n - i, n)
-            remote(
-                ctx_tx.at[r, origin], ctx_rx.at[r, origin], ctx_send.at[r, i - 1], ctx_recv.at[r, i - 1], at(origin)
-            ).wait_recv()
+
+    @pl.loop(1, n)
+    def _(i):
+        origin = lax.rem(me + n - i, n)
+        context_copy(i, origin, origin, origin).wait_recv()
 
     for c in range(CHUNKS):
         gw_load[c].start()
@@ -174,7 +169,7 @@
     for r in range(rows_here):
         for d in range(n):
             first = (d * rows_here + r) * heads_here
-            arrived = ctx_rx[r, d].astype(F32)
+            arrived = ctx_rx[d, r].astype(F32)
             for j in range(latent // 128):
                 ctx_rows[j, first : first + heads_here] = arrived[:, j * 128 : (j + 1) * 128]
     for h in range(heads_here):
@@ -353,10 +348,7 @@
     @pl.loop(1, n)
     def _(i):
         there = lax.rem(me + i, n)
-        for r in range(rows_here):
-            remote(
-                ctx_tx.at[r, there], ctx_rx.at[r, me], ctx_send.at[r, i - 1], ctx_recv.at[r, i - 1], at(there)
-            ).wait_send()
+        context_copy(i, there, me, there).wait_send()
         remote(cf_tx, cf_rx.at[me], cf_send.at[i - 1], cf_recv.at[i - 1], at(there)).wait_send()
 
     for copies in (copies_a, copies_b):
@@ -413,8 +405,8 @@
             vmem(gate_weight.shape[1:], BF16),
             vmem(up_weight.shape[1:], BF16),
             vmem(down_weight.shape[1:], BF16),
-            vmem((rows_here, n, heads_here, latent), BF16),
-            vmem((rows_here, n, heads_here, latent), BF16),
+            vmem((n, rows_here, heads_here, latent), BF16),
+            vmem((n, rows_here, heads_here, latent), BF16),
             vmem((latent // 128, rows * heads_here, 128), F32),
             vmem((rows, heads_here * value_size), BF16),
             vmem((rows_here, 128), F32),
@@ -436,8 +428,8 @@
             dma((CHUNKS,)),
             dma((CHUNKS,)),
             dma((CHUNKS,)),
-            dma((rows_here, n - 1)),
-            dma((rows_here, n - 1)),
+            dma((n - 1,)),
+            dma((n - 1,)),
             dma((n - 1,)),
             dma((n - 1,)),
             dma((2, CHUNKS, hops)),

time: 50.4 us -> 50 us (level)
  no operation moved by 1% of the time
where the time goes in v3:
time: 50 us; the launch traced here: 49.7 us
  Pallas kernels  48.3 us (97%)
  local copies, waits for them, and re-layouts  1.38 us (3%)
    pallas_call x1, Pallas kernels, on_device(): pl.pallas_call(functools.partial(layer_kernel, ep_n, side_n), out_shape=j...  48.3 us
    unnamed x1, local copies, waits for them, and re-layouts  1.38 us

profile of v3, /device:TPU:0, one launch (start us, length us, event | category | flops | bytes accessed | tf_op | source)
XLA Modules:
  0.0 49.7 jit_solution(6882293656787841242)
XLA Ops:
  0.0 48.3 %shard_map.118 = bf16[2,7168]{1,0:T(2,128)(2,1)} custom-call(s32[2]{0:T(128)} %lengths.1, s32[2,2]{1,0:T(2,128)} %ids.1, f32[2,2]{1,0:T(2,128)} %route.1, bf16[2,576,128]{2,1,0:T(8,128)(2,1)} %bitcast.4, bf16[2,576,256]{2,1,0:T(8,128)(2,1)} %bitcast.3, bf16[2,7168]{1,0:T(2,128)(2,1)} %resid.1, bf16[56,128]{1,0:T(8,128)(2,1)} %bitcast.5, ...), custom_call_target="tpu_custom_call" | custom-call | tf_op jit(solution)/shard_map/pallas_call | solution.py:395
  48.3 1.4 %copy.14 = bf16[2,7168]{1,0:T(2,128)(2,1)} copy(bf16[2,7168]{1,0:T(2,128)(2,1)} %shard_map.118) | data formatting | bytes 57344
